TPU v7x, 256 devices: a whole 4x4x8 slice. The times are simulated.
256 devices in a mesh: dp: 8 (over y_hi, x), tensor: 32 (over y_lo, z, core).
Axes of the slice: x: 4, y: 4 (y_hi: 2, y_lo: 2; y = y_hi * 2 + y_lo), z: 8, core: 2. Of those that a mesh axis runs over, the one named last changes fastest.
Arguments:
- tokens: bfloat16 [512, 9216], P('tensor', 'dp'), may hold values from -6 to 6
- w_in: bfloat16 [9216, 36864], P('dp', 'tensor'), may hold values from -0.0625 to 0.0625
- w_out: bfloat16 [36864, 9216], P('tensor', 'dp'), may hold values from -0.03125 to 0.03125
- cotangent: bfloat16 [512, 9216], P('tensor', 'dp'), may hold values from -6 to 6
Outputs:
- output: bfloat16 [512, 9216], P('tensor', 'dp')
- input_grad: bfloat16 [512, 9216], P('tensor', 'dp')
- w_in_grad: bfloat16 [9216, 36864], P('dp', 'tensor')
- w_out_grad: bfloat16 [36864, 9216], P('tensor', 'dp')
All inputs are finite; a program needn't handle non-finite values.
Results may differ from a plain program's by a relative error of at most 0.005.
Values may be sent and summed in bfloat16 or wider, within the bound.
A program may use at most 64 MiB of HBM per device.

v0:
```python
import math

import jax
import jax.numpy as jnp
from jax import lax
from jax.sharding import PartitionSpec as P


def gelu_value(v):
    return v * 0.5 * (1.0 + jax.scipy.special.erf(v / math.sqrt(2.0)))


def gelu_slope(v):
    cdf = 0.5 * (1.0 + jax.scipy.special.erf(v / math.sqrt(2.0)))
    return cdf + v * jnp.exp(-0.5 * v * v) / math.sqrt(2.0 * math.pi)


def contract_last(left, right):
    return lax.dot_general(
        left, right, (((1,), (1,)), ((), ())), preferred_element_type=jnp.float32
    )


def contract_first(left, right):
    return lax.dot_general(
        left, right, (((0,), (0,)), ((), ())), preferred_element_type=jnp.float32
    )


def on_device(tokens, w_in, w_out, cotangent):
    piece = lax.all_gather(tokens, "tensor", axis=0, tiled=True)
    partial_acc = jnp.dot(piece, w_in, preferred_element_type=jnp.float32)
    stored = piece
    hidden = lax.psum(partial_acc, "dp")
    activ = gelu_value(hidden).astype(jnp.bfloat16)
    rows = activ
    output = lax.psum_scatter(
        jnp.dot(rows, w_out, preferred_element_type=jnp.float32),
        "tensor",
        scatter_dimension=0,
        tiled=True,
    ).astype(jnp.bfloat16)
    piece = lax.all_gather(cotangent, "tensor", axis=0, tiled=True)
    grad_acc = contract_last(piece, w_out)
    w_out_grad = contract_first(activ, piece).astype(jnp.bfloat16)
    grad_activ = lax.psum(grad_acc, "dp")
    grad_hidden = (grad_activ * gelu_slope(hidden)).astype(jnp.bfloat16)
    rows = grad_hidden
    input_grad = lax.psum_scatter(
        contract_last(rows, w_in), "tensor", scatter_dimension=0, tiled=True
    ).astype(jnp.bfloat16)
    w_in_grad = contract_first(stored, grad_hidden).astype(jnp.bfloat16)
    return (output, input_grad, w_in_grad, w_out_grad)


def solution(mesh):
    in_specs = (P("tensor", "dp"), P("dp", "tensor"), P("tensor", "dp"), P("tensor", "dp"))
    out_specs = (P("tensor", "dp"), P("tensor", "dp"), P("dp", "tensor"), P("tensor", "dp"))
    return jax.shard_map(
        on_device, mesh=mesh, in_specs=in_specs, out_specs=out_specs, check_vma=False
    )
```

profile of v0, /device:TPU:1, one launch (start us, length us, event | category | flops | bytes accessed | tf_op | source)
XLA Modules:
  0.0 516.8 jit_solution(3689242389355878804)
XLA Ops:
  7.2 0.0 all-gather.5.cloned.1.call-start
  7.2 0.7 all-gather.5.cloned.1.call-update
  7.9 0.0 all-gather.3.cloned.1.call-start
  8.0 0.7 all-gather.3.cloned.1.call-update
  8.7 0.0 all-reduce.3.cloned.1.call-start
  8.7 69.4 %all-gather.5.cloned.1.call-done = bf16[512,1152]{1,0:T(8,128)(2,1)} async-done(((bf16[16,1152]{1,0:T(8,128)(2,1)}), bf16[512,1152]{1,0:T(8,128)(2,1)}) %all-gather.5.cloned.1.call-update) | async-done | bytes 1179664 | tf_op jit(solution)/shard_map/all_gather | solution.py:43
  78.1 5.4 %fusion.9 = f32[512,1152]{1,0:T(8,128)} fusion(bf16[512,1152]{1,0:T(8,128)(2,1)} %all-gather.5.cloned.1.call-done, bf16[1152,1152]{1,0:T(8,128)(2,1)} %param.6), kind=kOutput, calls=%fused_computation.14 | convolution fusion | flops 1358954496 | bytes 6193152 | tf_op jit(solution)/shard_map/dot_general | solution.py:19
  83.5 60.1 %all-gather.3.cloned.1.call-done = bf16[512,1152]{1,0:T(8,128)(2,1)} async-done(((bf16[16,1152]{1,0:T(8,128)(2,1)}), bf16[512,1152]{1,0:T(8,128)(2,1)}) %all-gather.3.cloned.1.call-update) | async-done | bytes 1179664 | tf_op jit(solution)/shard_map/all_gather | solution.py:31
  143.6 4.5 fusion.7
  148.2 0.0 reduce-scatter.5.cloned.1.call-start
  148.2 122.2 %all-reduce.3.cloned.1.call-done = (f32[512,1152]{1,0:T(8,128)}, f32[512,1152]{1,0:T(8,128)}) async-done(((f32[512,1152]{1,0:T(8,128)}, f32[512,1152]{1,0:T(8,128)}), (f32[512,1152]{1,0:T(8,128)}, f32[512,1152]{1,0:T(8,128)})) %all-reduce.3.cloned.1.call-update) | async-done | bytes 4718608 | tf_op jit(solution)/shard_map/psum | solution.py:34
  270.4 3.8 fusion.6
  274.2 1.0 copy-done.1
  275.2 3.3 fusion.10
  278.5 0.0 reduce-scatter.5.cloned.1.call-update
  278.5 0.0 reduce-scatter.3.cloned.1.call-start
  278.6 5.4 %fusion.8 = f32[512,1152]{1,0:T(8,128)} fusion(bf16[512,1152]{1,0:T(8,128)(2,1)} %get-tuple-element.11, bf16[1152,1152]{1,0:T(8,128)(2,1)} %param.6), kind=kOutput, calls=%fused_computation.13 | convolution fusion | flops 1358954496 | bytes 6193152 | tf_op jit(solution)/shard_map/dot_general | solution.py:38
  284.0 4.9 fusion
  288.8 5.2 %copy.8 = bf16[1152,1152]{1,0:T(8,128)(2,1)} copy(bf16[1152,1152]{0,1:T(8,128)(2,1)} %fusion) | data formatting | bytes 5308416
  294.1 4.9 convolution_convert_fusion
  298.9 92.7 %reduce-scatter.5.cloned.1.call-done = f32[16,1152]{1,0:T(8,128)} async-done(((f32[512,1152]{1,0:T(8,128)}), f32[16,1152]{1,0:T(8,128)}) %reduce-scatter.5.cloned.1.call-update) | async-done | bytes 73744 | tf_op jit(solution)/shard_map/reduce_scatter | solution.py:49
  391.6 1.5 convert_element_type.24
  393.1 115.6 %reduce-scatter.3.cloned.1.call-done = f32[16,1152]{1,0:T(8,128)} async-done(((f32[512,1152]{1,0:T(8,128)}), f32[16,1152]{1,0:T(8,128)}) %reduce-scatter.3.cloned.1.call-update) | async-done | bytes 73744 | tf_op jit(solution)/shard_map/reduce_scatter | solution.py:37
  508.7 1.5 convert_element_type.22
  (5 shorter events, 0.0 us)
Async XLA Ops:
  7.2 136.5 %copy-start = (bf16[1152,1152]{1,0:T(8,128)(2,1)S(1)}, bf16[1152,1152]{1,0:T(8,128)(2,1)}, u32[]{:S(2)}) copy-start(bf16[1152,1152]{1,0:T(8,128)(2,1)} %param.5) | copy-start | bytes 7962628
  7.2 70.9 %all-gather.5.cloned.1.call-start = ((), (), s32[]{:S(2)}) async-start(), calls=%async_computation.4 | async-start | bytes 1216512 | tf_op jit(solution)/shard_map/all_gather | solution.py:43
  7.9 135.7 %all-gather.3.cloned.1.call-start = ((), (), s32[]{:S(2)}) async-start(), calls=%async_computation.2 | async-start | bytes 1216512 | tf_op jit(solution)/shard_map/all_gather | solution.py:31
  8.7 261.8 %all-reduce.3.cloned.1.call-start = ((), (), s32[]{:S(2)}) async-start(), calls=%async_computation.6 | async-start | bytes 9437184 | tf_op jit(solution)/shard_map/psum | solution.py:34
  148.2 243.5 %reduce-scatter.5.cloned.1.call-start = ((), (), s32[]{:S(2)}) async-start(), calls=%async_computation.5 | async-start | bytes 2433024 | tf_op jit(solution)/shard_map/reduce_scatter | solution.py:49
  274.2 1.0 copy-start.1
  278.5 230.2 %reduce-scatter.3.cloned.1.call-start = ((), (), s32[]{:S(2)}) async-start(), calls=%async_computation.3 | async-start | bytes 2433024 | tf_op jit(solution)/shard_map/reduce_scatter | solution.py:37
Sparse Core Ops, SparseCore 0:
  9.9 68.1 all-gather.4
  80.0 63.6 all-gather.2
  148.3 122.0 all-reduce.2
  278.7 112.9 reduce-scatter.4
  394.0 114.6 reduce-scatter.2
where the time goes:
time: 520 us; the launch traced here: 517 us
  waiting for transfers between devices  461 us (89%)
  matrix products  28.3 us (5%)
  between operations  13.8 us (3%)
  other arithmetic  6.8 us (1%)
  local copies, waits for them, and re-layouts  6.25 us (1%)
    psum x1, waiting for transfers between devices, on_device(): hidden = lax.psum(partial_acc, 'dp')  122 us
    reduce_scatter x1, waiting for transfers between devices, on_device(): lax.psum_scatter(jnp.dot(rows, w_out, preferred_element_type=jnp.float32)...  116 us
    reduce_scatter x1, waiting for transfers between devices, on_device(): lax.psum_scatter(contract_last(rows, w_in), 'tensor', scatter_dimension=0...  92.7 us
    all_gather x1, waiting for transfers between devices, on_device(): piece = lax.all_gather(cotangent, 'tensor', axis=0, tiled=True)  69.4 us
    all_gather x1, waiting for transfers between devices, on_device(): piece = lax.all_gather(tokens, 'tensor', axis=0, tiled=True)  60.1 us
  transfers between devices with their start and end apart: 5, of which 5 were waited for; matrix products, arithmetic and copies ran while one was open for 5% of the time, Pallas kernels for 0%

commit v1 on v0

v1 whole, which is shorter than its diff:
```python
import functools
import math

import jax
import jax.numpy as jnp
from jax import lax
from jax.experimental import pallas as pl
from jax.experimental.pallas import tpu as pltpu
from jax.sharding import PartitionSpec as P

MESH = pl.DeviceIdType.MESH
ROWS = 512
W = 1152
OWN = 16
NX, NYH, NYL, NZ, NC = 4, 2, 2, 8, 2
NB = 4
RB = ROWS // NB
KO = NZ // NB
XR = RB // NX
YR = XR // NYH
OFFSETS = [[0, 1], [7, 2], [6, 3], [5, 4]]
TN = 384
N_MSG = 256


def gelu_value(v):
    return v * 0.5 * (1.0 + lax.erf(v * (1.0 / math.sqrt(2.0))))


def gelu_slope(v):
    cdf = 0.5 * (1.0 + lax.erf(v * (1.0 / math.sqrt(2.0))))
    return cdf + v * jnp.exp(-0.5 * v * v) * (1.0 / math.sqrt(2.0 * math.pi))


def block_kernel(
    tok_hbm, win_hbm, wout_hbm, cot_hbm,
    out_ref, ing_ref, t_out, c_out, a_out, g_out,
    win, wout, acts, part, sendp, xrecv, ysend, yrecv, ownp, slopes, mids,
    core_send, core_recv, tens_part, ylo_send, ylo_recv, fin_own, zsend, zrecv,
    local_sem, send_sem, recv_sem,
):
    d, t = lax.axis_index("dp"), lax.axis_index("tensor")
    yh, x = d // NX, d % NX
    yl, z, c = t // (NZ * NC), (t // NC) % NZ, t % NC

    def at_x(s):
        return {"dp": yh * NX + (x + s) % NX}

    def at_z(s):
        return {"tensor": yl * (NZ * NC) + ((z + s) % NZ) * NC + c}

    y_hi = {"dp": (1 - yh) * NX + x}
    y_lo = {"tensor": (1 - yl) * (NZ * NC) + z * NC + c}
    core = {"tensor": t + 1 - 2 * c}

    loads = [
        pltpu.make_async_copy(tok_hbm, acts.at[0, pl.ds(0, OWN)], local_sem.at[0]),
        pltpu.make_async_copy(cot_hbm, acts.at[1, pl.ds(0, OWN)], local_sem.at[1]),
        pltpu.make_async_copy(win_hbm, win, local_sem.at[2]),
        pltpu.make_async_copy(wout_hbm, wout, local_sem.at[3]),
    ]
    for load in loads:
        load.start()

    barrier = pltpu.get_barrier_semaphore()
    partners = [at_x(s) for s in (1, 2, 3)] + [y_hi, y_lo, core]
    partners += [at_z(s) for s in range(1, NZ)]
    for partner in partners:
        pl.semaphore_signal(barrier, inc=1, device_id=partner, device_id_type=MESH)
    pl.semaphore_wait(barrier, len(partners))

    messages = {}

    def send(key, src, dst, to):
        i = len(messages)
        messages[key] = pltpu.make_async_remote_copy(
            src_ref=src,
            dst_ref=dst,
            send_sem=send_sem.at[i],
            recv_sem=recv_sem.at[i],
            device_id=to,
            device_id_type=MESH,
        )
        messages[key].start()

    def arrived(*key):
        messages[key].wait_recv()

    def rows_at(b, ry, rc, k=0):
        return b * RB + ry * (RB // 2) + rc * (RB // 4) + k * OWN

    def gather_z(s):
        loads[s].wait()
        for b in range(NB):
            for k, o in enumerate(OFFSETS[b]):
                if o:
                    send(
                        ("gz", s, b, k),
                        acts.at[s, pl.ds(0, OWN)],
                        acts.at[s, pl.ds(rows_at(b, 0, 0, k), OWN)],
                        at_z(-o + NZ),
                    )

    def gather_y(b, s):
        for k, o in enumerate(OFFSETS[b]):
            if o:
                arrived("gz", s, b, k)
        n = KO * OWN
        src = acts.at[s, pl.ds(rows_at(b, 0, 0), n)]
        send(("gy", s, b), src, acts.at[s, pl.ds(rows_at(b, 1, 0), n)], y_lo)
        send(("gc", s, b, 0), src, acts.at[s, pl.ds(rows_at(b, 0, 1), n)], core)

    def gather_c(b, s):
        n = KO * OWN
        arrived("gy", s, b)
        src = acts.at[s, pl.ds(rows_at(b, 1, 0), n)]
        send(("gc", s, b, 1), src, acts.at[s, pl.ds(rows_at(b, 1, 1), n)], core)

    def x_rows(b, xi):
        return pl.ds(pl.multiple_of(b * RB + xi * XR, XR), XR)

    def own_rows(b, xi, yi):
        return pl.ds(pl.multiple_of(b * RB + xi * XR + yi * YR, YR), YR)

    def first_product(b, s):
        arrived("gc", s, b, 0)
        arrived("gc", s, b, 1)
        if s == 0 and b < 2:
            loads[2 + b].wait()
        left = acts[s, pl.ds(b * RB, RB), :]
        for n in range(0, W, TN):
            if s == 0:
                part[:, pl.ds(n, TN)] = jnp.dot(
                    left, win[:, pl.ds(n, TN)], preferred_element_type=jnp.float32
                )
            else:
                part[:, pl.ds(n, TN)] = lax.dot_general(
                    left, wout[pl.ds(n, TN), :], (((1,), (1,)), ((), ())),
                    preferred_element_type=jnp.float32,
                )
        sendp[s, pl.ds(b * RB, RB), :] = part[...].astype(jnp.bfloat16)
        for h in (2, 1, 3):
            send(
                ("rx", s, b, h),
                sendp.at[s, x_rows(b, (x + h) % NX)],
                xrecv.at[s, b, h - 1],
                at_x(h),
            )
        ownp[s, b] = part[pl.ds(pl.multiple_of(x * XR, XR), XR), :]

    def reduce_x(b, s):
        for h in (1, 2, 3):
            arrived("rx", s, b, h)
        total = ownp[s, b]
        for h in range(3):
            total = total + xrecv[s, b, h].astype(jnp.float32)
        ownp[s, b] = total
        other = ownp[s, b, pl.ds(pl.multiple_of((1 - yh) * YR, YR), YR), :]
        ysend[s, b] = other.astype(jnp.bfloat16)
        send(("ry", s, b), ysend.at[s, b], yrecv.at[s, b], y_hi)

    def middle(b, s):
        arrived("ry", s, b)
        mine = ownp[s, b, pl.ds(pl.multiple_of(yh * YR, YR), YR), :]
        total = mine + yrecv[s, b].astype(jnp.float32)
        if s == 0:
            value = gelu_value(total)
            slopes[b] = gelu_slope(total)
        else:
            value = total * slopes[b]
        rows = own_rows(b, x, yh)
        mids[s, rows, :] = value.astype(jnp.bfloat16)
        here = mids.at[s, rows]
        send(("ay", s, b), here, here, y_hi)
        for h in (2, 1, 3):
            send(("ax", s, b, h), here, here, at_x(h))

    def forward(b, s):
        arrived("ay", s, b)
        here = mids.at[s, own_rows(b, x, 1 - yh)]
        for h in (2, 1, 3):
            send(("af", s, b, h), here, here, at_x(h))

    def second_product(b, s):
        for h in (1, 2, 3):
            arrived("ax", s, b, h)
            arrived("af", s, b, h)
        left = mids[s, pl.ds(b * RB, RB), :]
        for n in range(0, W, TN):
            if s == 0:
                tens_part[:, pl.ds(n, TN)] = jnp.dot(
                    left, wout[:, pl.ds(n, TN)], preferred_element_type=jnp.float32
                )
            else:
                tens_part[:, pl.ds(n, TN)] = lax.dot_general(
                    left, win[pl.ds(n, TN), :], (((1,), (1,)), ((), ())),
                    preferred_element_type=jnp.float32,
                )
        q = RB // 4
        for ry in range(2):
            core_send[s, b, ry] = tens_part[pl.ds(rows_at(0, ry, 1), q), :]
            core_recv[s, b, 2 + ry] = tens_part[pl.ds(rows_at(0, ry, 0), q), :]
        send(("oc", s, b), core_send.at[s, b], core_recv.at[s, b, pl.ds(0, 2)], core)

    def reduce_c(b, s):
        arrived("oc", s, b)
        ylo_send[s, b] = (core_recv[s, b, 1] + core_recv[s, b, 3]).astype(jnp.bfloat16)
        core_recv[s, b, 2] = core_recv[s, b, 0] + core_recv[s, b, 2]
        send(("oy", s, b), ylo_send.at[s, b], ylo_recv.at[s, b], y_lo)

    def reduce_y(b, s):
        arrived("oy", s, b)
        total = core_recv[s, b, 2] + ylo_recv[s, b].astype(jnp.float32)
        for k, o in enumerate(OFFSETS[b]):
            rows = total[k * OWN : (k + 1) * OWN]
            if o == 0:
                fin_own[s] = rows
            else:
                zsend[s, o] = rows.astype(jnp.bfloat16)
                send(("oz", s, o), zsend.at[s, o], zrecv.at[s, o], at_z(o))

    def finish(s):
        total = fin_own[s]
        for o in range(1, NZ):
            arrived("oz", s, o)
            total = total + zrecv[s, o].astype(jnp.float32)
        if s == 0:
            out_ref[...] = total.astype(jnp.bfloat16)
        else:
            ing_ref[...] = total.astype(jnp.bfloat16)

    gather_z(0)
    gather_z(1)
    items = [(b, s) for s in range(2) for b in range(NB)]
    stages = [
        lambda b, s: gather_y(b, s),
        lambda b, s: gather_c(b, s),
        first_product,
        reduce_x,
        middle,
        forward,
        second_product,
        reduce_c,
        reduce_y,
    ]
    saves = []

    def save(src, dst):
        saves.append(pltpu.make_async_copy(src, dst, local_sem.at[4 + len(saves)]))
        saves[-1].start()

    n_items, n_stages = len(items), len(stages)
    for slot in range(n_items + n_stages - 1):
        for k in reversed(range(n_stages)):
            i = slot - k
            if 0 <= i < n_items:
                b, s = items[i]
                stages[k](b, s)
                if k == 2 and b == NB - 1:
                    save(acts.at[s], (t_out, c_out)[s])
                if k == 6 and b == NB - 1:
                    save(mids.at[s], (a_out, g_out)[s])
    finish(0)
    finish(1)
    for copy in saves:
        copy.wait()
    for copy in messages.values():
        copy.wait_send()


def block(tokens, w_in, w_out, cotangent):
    bf16, f32 = jnp.bfloat16, jnp.float32
    any_space = pl.BlockSpec(memory_space=pl.ANY)
    vmem = pl.BlockSpec(memory_space=pltpu.VMEM)
    wide = jax.ShapeDtypeStruct((ROWS, W), bf16)
    own = jax.ShapeDtypeStruct((OWN, W), bf16)
    q = RB // 4
    return pl.pallas_call(
        block_kernel,
        out_shape=(own, own, wide, wide, wide, wide),
        in_specs=[any_space] * 4,
        out_specs=(vmem, vmem) + (any_space,) * 4,
        scratch_shapes=[
            pltpu.VMEM((W, W), bf16),
            pltpu.VMEM((W, W), bf16),
            pltpu.VMEM((2, ROWS, W), bf16),
            pltpu.VMEM((RB, W), f32),
            pltpu.VMEM((2, ROWS, W), bf16),
            pltpu.VMEM((2, NB, 3, XR, W), bf16),
            pltpu.VMEM((2, NB, YR, W), bf16),
            pltpu.VMEM((2, NB, YR, W), bf16),
            pltpu.VMEM((2, NB, XR, W), f32),
            pltpu.VMEM((NB, YR, W), f32),
            pltpu.VMEM((2, ROWS, W), bf16),
            pltpu.VMEM((2, NB, 2, q, W), f32),
            pltpu.VMEM((2, NB, 4, q, W), f32),
            pltpu.VMEM((RB, W), f32),
            pltpu.VMEM((2, NB, q, W), bf16),
            pltpu.VMEM((2, NB, q, W), bf16),
            pltpu.VMEM((2, OWN, W), f32),
            pltpu.VMEM((2, NZ, OWN, W), bf16),
            pltpu.VMEM((2, NZ, OWN, W), bf16),
            pltpu.SemaphoreType.DMA((8,)),
            pltpu.SemaphoreType.DMA((N_MSG,)),
            pltpu.SemaphoreType.DMA((N_MSG,)),
        ],
        compiler_params=pltpu.CompilerParams(
            collective_id=0, has_side_effects=True, vmem_limit_bytes=56 << 20
        ),
        cost_estimate=pl.CostEstimate(
            flops=8 * ROWS * W * W, bytes_accessed=10 << 20, transcendentals=0
        ),
        name="mlp_block",
    )(tokens, w_in, w_out, cotangent)


def weight_grads_kernel(t_ref, g_ref, a_ref, c_ref, win_grad, wout_grad):
    for left, right, out in ((t_ref, g_ref, win_grad), (a_ref, c_ref, wout_grad)):
        out[...] = lax.dot_general(
            left[...], right[...], (((0,), (0,)), ((), ())),
            preferred_element_type=jnp.float32,
        ).astype(jnp.bfloat16)


def weight_grads(t, g, a, c):
    tm = 128
    whole = pl.BlockSpec((ROWS, W), lambda i: (0, 0))
    piece = pl.BlockSpec((ROWS, tm), lambda i: (0, i))
    out = pl.BlockSpec((tm, W), lambda i: (i, 0))
    return pl.pallas_call(
        weight_grads_kernel,
        grid=(W // tm,),
        out_shape=(jax.ShapeDtypeStruct((W, W), jnp.bfloat16),) * 2,
        in_specs=[piece, whole, piece, whole],
        out_specs=(out, out),
        compiler_params=pltpu.CompilerParams(vmem_limit_bytes=32 << 20),
        name="weight_grads",
    )(t, g, a, c)


def on_device(tokens, w_in, w_out, cotangent):
    output, input_grad, t, c, a, g = block(tokens, w_in, w_out, cotangent)
    w_in_grad, w_out_grad = weight_grads(t, g, a, c)
    return (output, input_grad, w_in_grad, w_out_grad)


def solution(mesh):
    in_specs = (P("tensor", "dp"), P("dp", "tensor"), P("tensor", "dp"), P("tensor", "dp"))
    out_specs = (P("tensor", "dp"), P("tensor", "dp"), P("dp", "tensor"), P("tensor", "dp"))
    return jax.shard_map(
        on_device, mesh=mesh, in_specs=in_specs, out_specs=out_specs, check_vma=False
    )
```

time: 520 us -> 111 us (0.21)
  waiting for transfers between devices: 461 us -> 0 us
  Pallas kernels: 0 us -> 104 us
  matrix products: 28.3 us -> 0 us
  between operations: 13.8 us -> 0.65 us
  other arithmetic: 6.8 us -> 0 us
    reduce_scatter x2 -> x0, waiting for transfers between devices: 208 us -> none  [the longest x1 116 us: on_device(): lax.psum_scatter(jnp.dot(rows, w_out, preferred_element_type=jnp.float32)...]
    all_gather x2 -> x0, waiting for transfers between devices: 130 us -> none  [the longest x1 69.4 us: on_device(): piece = lax.all_gather(cotangent, 'tensor', axis=0, tiled=True)]
    psum x1 -> x0, waiting for transfers between devices: 122 us -> none  [on_device(): hidden = lax.psum(partial_acc, 'dp')]
    pallas_call x0 -> x2, Pallas kernels: none -> 104 us  [the longest x1 97.2 us: block(): pl.pallas_call(block_kernel, out_shape=(own, own, wide, wide, wide, wide)...]
    dot_general x6 -> x0, matrix products: 28.3 us -> none  [the longest x2 9.73 us: contract_first(): lax.dot_general(left, right, (((0,), (0,)), ((), ())), preferred_element_...]
    convert_element_type x3 -> x0, other arithmetic: 6.8 us -> none  [the longest x1 3.79 us: on_device(): grad_hidden = (grad_activ * gelu_slope(hidden)).astype(jnp.bfloat16)]
  transfers between devices with their start and end apart: 5 -> 0, of which waited for: 5 -> 0; matrix products, arithmetic and copies ran while one was open for 5% -> 0% of each run, Pallas kernels for 0% -> 0%
where the time goes in v1:
time: 111 us
  Pallas kernels  104 us (94%)
  local copies, waits for them, and re-layouts  6.31 us (6%)
    pallas_call x1, Pallas kernels, block(): pl.pallas_call(block_kernel, out_shape=(own, own, wide, wide, wide, wide)...  97.2 us
    pallas_call x1, Pallas kernels, weight_grads(): pl.pallas_call(weight_grads_kernel, grid=(W // tm,), out_shape=(jax.Shape...  6.55 us
    unnamed x14, local copies, waits for them, and re-layouts  6.31 us

profile of v1, /device:TPU:1, one launch (start us, length us, event | category | flops | bytes accessed | tf_op | source)
XLA Modules:
  0.0 110.7 jit_solution(5161107966507376181)
XLA Ops:
  0.6 97.2 %mlp_block.1 = (bf16[16,1152]{1,0:T(8,128)(2,1)}, bf16[16,1152]{1,0:T(8,128)(2,1)}, bf16[512,1152]{1,0:T(8,128)(2,1)}, bf16[512,1152]{1,0:T(8,128)(2,1)}, bf16[5...) custom-call(bf16[16,1152]{1,0:T(8,128)(2,1)} %tok_hbm.1, bf16[1152,1152]{1,0:T(8,128)(2,1)} %win_hbm.1, ...), custom_call_target="tpu_custom_call" | custom-call | flops 5435817984 | bytes 10485760 | tf_op jit(solution)/shard_map/mlp_block/pallas_call | solution.py:278
  97.8 0.0 copy-start
  97.8 1.3 %copy-done = bf16[512,1152]{1,0:T(8,128)(2,1)S(1)} copy-done((bf16[512,1152]{1,0:T(8,128)(2,1)S(1)}, bf16[512,1152]{1,0:T(8,128)(2,1)}, u32[]{:S(2)}) %copy-start) | copy-done | bytes 1179672
  99.1 0.0 copy-start.1
  99.1 1.3 %copy-done.1 = bf16[512,1152]{1,0:T(8,128)(2,1)S(1)} copy-done((bf16[512,1152]{1,0:T(8,128)(2,1)S(1)}, bf16[512,1152]{1,0:T(8,128)(2,1)}, u32[]{:S(2)}) %copy-start.1) | copy-done | bytes 1179672
  100.3 0.0 copy-start.2
  100.4 1.3 %copy-done.2 = bf16[512,1152]{1,0:T(8,128)(2,1)S(1)} copy-done((bf16[512,1152]{1,0:T(8,128)(2,1)S(1)}, bf16[512,1152]{1,0:T(8,128)(2,1)}, u32[]{:S(2)}) %copy-start.2) | copy-done | bytes 1179672
  101.6 0.0 copy-start.3
  101.6 1.3 %copy-done.3 = bf16[512,1152]{1,0:T(8,128)(2,1)S(1)} copy-done((bf16[512,1152]{1,0:T(8,128)(2,1)S(1)}, bf16[512,1152]{1,0:T(8,128)(2,1)}, u32[]{:S(2)}) %copy-start.3) | copy-done | bytes 1179672
  102.9 0.0 copy-start.5
  102.9 0.0 copy-start.4
  102.9 6.5 %weight_grads.1 = (bf16[1152,1152]{1,0:T(8,128)(2,1)}, bf16[1152,1152]{1,0:T(8,128)(2,1)}) custom-call(bf16[512,1152]{1,0:T(8,128)(2,1)S(1)} %copy-done, bf16[512,1152]{1,0:T(8,128)(2,1)S(1)} %copy-done.3, bf16[512,1152]{1,0:T(8,128)(2,1)S(1)} %copy-done.2, bf16[512,1152]{1,0:T(8,128)(2,1)S(1)} %copy-done.1), custom_call_target="tpu_custom_call" | custom-call | tf_op jit(solution)/shard_map/weight_grads/pallas_call | solution.py:330
  109.4 0.0 copy-done.5
  109.4 0.6 copy.10
  110.1 0.0 copy-done.4
  110.1 0.6 copy.11
Async XLA Ops:
  97.8 1.3 %copy-start = (bf16[512,1152]{1,0:T(8,128)(2,1)S(1)}, bf16[512,1152]{1,0:T(8,128)(2,1)}, u32[]{:S(2)}) copy-start(bf16[512,1152]{1,0:T(8,128)(2,1)} %get-tuple-element.14.t_ref) | copy-start | bytes 3538948
  99.1 1.3 %copy-start.1 = (bf16[512,1152]{1,0:T(8,128)(2,1)S(1)}, bf16[512,1152]{1,0:T(8,128)(2,1)}, u32[]{:S(2)}) copy-start(bf16[512,1152]{1,0:T(8,128)(2,1)} %get-tuple-element.17.c_ref) | copy-start | bytes 3538948
  100.3 1.3 %copy-start.2 = (bf16[512,1152]{1,0:T(8,128)(2,1)S(1)}, bf16[512,1152]{1,0:T(8,128)(2,1)}, u32[]{:S(2)}) copy-start(bf16[512,1152]{1,0:T(8,128)(2,1)} %get-tuple-element.16.a_ref) | copy-start | bytes 3538948
  101.6 1.3 %copy-start.3 = (bf16[512,1152]{1,0:T(8,128)(2,1)S(1)}, bf16[512,1152]{1,0:T(8,128)(2,1)}, u32[]{:S(2)}) copy-start(bf16[512,1152]{1,0:T(8,128)(2,1)} %get-tuple-element.15.g_ref) | copy-start | bytes 3538948
  102.9 6.6 %copy-start.5 = (bf16[16,1152]{1,0:T(8,128)(2,1)S(1)}, bf16[16,1152]{1,0:T(8,128)(2,1)}, u32[]{:S(2)}) copy-start(bf16[16,1152]{1,0:T(8,128)(2,1)} %get-tuple-element.24) | copy-start | bytes 110596
  102.9 7.2 %copy-start.4 = (bf16[16,1152]{1,0:T(8,128)(2,1)S(1)}, bf16[16,1152]{1,0:T(8,128)(2,1)}, u32[]{:S(2)}) copy-start(bf16[16,1152]{1,0:T(8,128)(2,1)} %get-tuple-element.25) | copy-start | bytes 110596

commit v2 on v0

v2 whole, which is shorter than its diff:
```python
import functools
import math

import jax
import jax.numpy as jnp
from jax import lax
from jax.experimental import pallas as pl
from jax.experimental.pallas import tpu as pltpu
from jax.sharding import PartitionSpec as P

MESH = pl.DeviceIdType.MESH
ROWS = 512
W = 1152
OWN = 16
NX, NYH, NYL, NZ, NC = 4, 2, 2, 8, 2
NB = 4
RB = ROWS // NB
KO = NZ // NB
XR = RB // NX
YR = XR // NYH
OFFSETS = [[0, 1], [7, 2], [6, 3], [5, 4]]
Q = RB // 4
TN = 384
TM = 128
N_LAND, N_LEAVE = 95, 13


def gelu_value(v):
    return v * 0.5 * (1.0 + lax.erf(v * (1.0 / math.sqrt(2.0))))


def gelu_slope(v):
    cdf = 0.5 * (1.0 + lax.erf(v * (1.0 / math.sqrt(2.0))))
    return cdf + v * jnp.exp(-0.5 * v * v) * (1.0 / math.sqrt(2.0 * math.pi))

LAG_GATHER_Y, LAG_GATHER_C = -1.5, -0.1
GATHER_Y_1, GATHER_C_1 = -1.5, -0.1
LAG_PASS_ON, LAG_REDUCE_X, LAG_MIDDLE = 1.9, 3.8, 5.7
LAG_FORWARD_Y, LAG_FORWARD_X, LAG_SECOND = 7.6, 9.5, 11.5
LAG_REDUCE_C, LAG_REDUCE_Y = 12.4, 14.3
FINISH_0 = 20.0
GRAD_AT_1 = [15.45 + 0.5 * m for m in range(W // TM)]
GRAD_AT_0 = [19.46] * 3 + [20.5] * 6
GATHER_1 = -0.05
DIRECT_GATHER = {(0, 0), (1, 0)}
DIRECT_REDUCE = {(0, 1)}
DIAGONAL = {
    f % NZ for b, _ in DIRECT_GATHER | DIRECT_REDUCE for o in OFFSETS[b] for f in (o, -o) if o
}


def block_kernel(
    tok_hbm, win_hbm, wout_hbm, cot_hbm,
    out_ref, ing_ref, wing_ref, woutg_ref,
    win, wout, acts, part, sendp, xrecv, ysend, yrecv, ownp, slopes, mids,
    core_send, core_recv, core_own, tens_part, ylo_send, ylo_recv,
    fin_own, zsend, zrecv, local_sem, send_sem, recv_sem,
):
    bf16, f32 = jnp.bfloat16, jnp.float32
    d, t = lax.axis_index("dp"), lax.axis_index("tensor")
    yh, x = d // NX, d % NX
    yl, z, c = t // (NZ * NC), (t // NC) % NZ, t % NC

    def at_x(s):
        return {"dp": yh * NX + (x + s) % NX}

    def at_z(s, ry=0):
        y = yl if ry == 0 else 1 - yl
        return {"tensor": y * (NZ * NC) + ((z + s) % NZ) * NC + c}

    y_hi = {"dp": (1 - yh) * NX + x}
    core = {"tensor": t + 1 - 2 * c}

    loads = [
        pltpu.make_async_copy(tok_hbm, acts.at[0, pl.ds(0, OWN)], local_sem.at[0]),
        pltpu.make_async_copy(cot_hbm, acts.at[1, pl.ds(0, OWN)], local_sem.at[1]),
        pltpu.make_async_copy(win_hbm, win, local_sem.at[2]),
        pltpu.make_async_copy(wout_hbm, wout, local_sem.at[3]),
    ]
    for load in loads:
        load.start()

    barrier = pltpu.get_barrier_semaphore()
    partners = [at_x(1), at_x(3), y_hi, core, at_z(0, 1)]
    partners += [at_z(s) for s in range(1, NZ)]
    partners += [at_z(s, 1) for s in sorted(DIAGONAL)]
    for partner in partners:
        pl.semaphore_signal(barrier, inc=1, device_id=partner, device_id_type=MESH)
    pl.semaphore_wait(barrier, len(partners))

    landing, leaving = {}, {}

    def send(group, src, dst, to, rows, unit=1):
        kind = group[0]
        i = landing.setdefault(group, [len(landing), 0])
        j = leaving.setdefault(kind, [len(leaving), 0])
        i[1] += rows * unit
        j[1] += rows * unit
        pltpu.make_async_remote_copy(
            src_ref=src,
            dst_ref=dst,
            send_sem=send_sem.at[j[0]],
            recv_sem=recv_sem.at[i[0]],
            device_id=to,
            device_id_type=MESH,
        ).start()

    def bytes_of(rows):
        if rows <= ROWS:
            return acts.at[0, pl.ds(0, rows)]
        if rows == 2 * NB * 6 * YR:
            return xrecv
        assert rows == 2 * NB * 4 * Q, rows
        return core_send

    def arrived(*group):
        i, rows = landing[group]
        view = bytes_of(rows)
        pltpu.make_async_remote_copy(
            view, view, send_sem.at[0], recv_sem.at[i], device_id=core, device_id_type=MESH
        ).wait_recv()

    def all_left():
        for i, rows in leaving.values():
            view = bytes_of(rows)
            pltpu.make_async_remote_copy(
                view, view, send_sem.at[i], recv_sem.at[0], device_id=core, device_id_type=MESH
            ).wait_send()

    def rows_at(b, rc, ry, k=0):
        return b * RB + rc * (RB // 2) + ry * (RB // 4) + k * OWN

    def start_gather(s, blocks):
        loads[s].wait()
        src = acts.at[s, pl.ds(0, OWN)]
        for b in blocks:
            for k, o in enumerate(OFFSETS[b]):
                for ry in range(2):
                    if (o or ry) and (ry == 0 or (b, s) in DIRECT_GATHER):
                        dst = acts.at[s, pl.ds(rows_at(b, 0, ry, k), OWN)]
                        send(("gz", s, b), src, dst, at_z(NZ - o, ry), OWN)

    def gather_y(b, s):
        if (b, s) in DIRECT_GATHER:
            return
        arrived("gz", s, b)
        src = acts.at[s, pl.ds(rows_at(b, 0, 0), Q)]
        send(("gy", s, b), src, acts.at[s, pl.ds(rows_at(b, 0, 1), Q)], at_z(0, 1), Q)

    def gather_c(b, s):
        arrived("gz" if (b, s) in DIRECT_GATHER else "gy", s, b)
        src = acts.at[s, pl.ds(rows_at(b, 0, 0), 2 * Q)]
        send(("gc", s, b), src, acts.at[s, pl.ds(rows_at(b, 1, 0), 2 * Q)], core, 2 * Q)

    def half(b, xi, yi):
        return pl.ds(pl.multiple_of(b * RB + xi * XR + yi * YR, YR), YR)

    def first_product(b, s):
        arrived("gc", s, b)
        if s == 0 and b < 2:
            loads[2 + b].wait()
        left = acts[s, pl.ds(b * RB, RB), :]
        for n in range(0, W, TN):
            cols = pl.ds(n, TN)
            if s == 0:
                part[s, b, :, cols] = jnp.dot(left, win[:, cols], preferred_element_type=f32)
            else:
                part[s, b, :, cols] = lax.dot_general(
                    left, wout[cols, :], (((1,), (1,)), ((), ())), preferred_element_type=f32
                )
        sendp[s, pl.ds(b * RB, RB), :] = part[s, b].astype(bf16)

        def send_half(group, xi, yi, slot, to):
            src = sendp.at[s, half(b, xi % NX, yi)]
            send((group, s, b), src, xrecv.at[s, b, slot], to, YR)

        send_half("r1", x + 2, 0, 0, at_x(1))
        send_half("r1", x + 2, 1, 1, at_x(3))
        send_half("r2", x + 1, 1, 2, at_x(1))
        send_half("r2", x + 3, 0, 3, at_x(3))

    def pass_on(b, s):
        arrived("r1", s, b)
        for i, step in ((0, 1), (1, 3)):
            there = (x + step) % NX
            mine = part[s, b, half(0, there, i), :]
            rows = half(b, there, i)
            sendp[s, rows, :] = (mine + xrecv[s, b, i].astype(f32)).astype(bf16)
            send(("r2", s, b), sendp.at[s, rows], xrecv.at[s, b, 4 + i], at_x(step), YR)

    def reduce_x(b, s):
        arrived("r2", s, b)
        for i in range(2):
            near = xrecv[s, b, 3 - i].astype(f32) + xrecv[s, b, 4 + i].astype(f32)
            ownp[s, b, i] = part[s, b, half(0, x, i), :] + near
        ysend[s, b] = ownp[s, b, 1 - yh].astype(bf16)
        send(("ry", s, b), ysend.at[s, b], yrecv.at[s, b], y_hi, YR)

    def middle(b, s):
        arrived("ry", s, b)
        total = ownp[s, b, yh] + yrecv[s, b].astype(f32)
        if s == 0:
            value = gelu_value(total)
            slopes[b] = gelu_slope(total)
        else:
            value = total * slopes[b]
        rows = half(b, x, yh)
        mids[s, rows, :] = value.astype(bf16)
        here = mids.at[s, rows]
        send(("ay", s, b), here, here, y_hi, YR)
        send(("a1", s, b), here, here, at_x(1), YR)
        send(("a3", s, b), here, here, at_x(3), YR)

    def forward_y(b, s):
        arrived("ay", s, b)
        here = mids.at[s, half(b, x, 1 - yh)]
        send(("a3", s, b), here, here, at_x(1), YR)
        send(("a2", s, b), here, here, at_x(3), YR)

    def forward_x(b, s):
        arrived("a1", s, b)
        here = mids.at[s, half(b, (x + 3) % NX, yh)]
        send(("a3", s, b), here, here, at_x(1), YR)
        arrived("a2", s, b)
        here = mids.at[s, half(b, (x + 1) % NX, 1 - yh)]
        send(("a3", s, b), here, here, at_x(3), YR)

    def second_product(b, s):
        arrived("a3", s, b)
        left = mids[s, pl.ds(b * RB, RB), :]
        for n in range(0, W, TN):
            cols = pl.ds(n, TN)
            if s == 0:
                tens_part[:, cols] = jnp.dot(left, wout[:, cols], preferred_element_type=f32)
            else:
                tens_part[:, cols] = lax.dot_general(
                    left, win[cols, :], (((1,), (1,)), ((), ())), preferred_element_type=f32
                )
        core_send[s, b] = tens_part[pl.ds(2 * Q, 2 * Q), :]
        core_own[s, b] = tens_part[pl.ds(0, 2 * Q), :]
        send(("oc", s, b), core_send.at[s, b], core_recv.at[s, b], core, 2 * Q, 2)

    def send_z(s, o, ry, rows):
        i = 2 * o + ry
        zsend[s, i] = rows.astype(bf16)
        send(("oz", s), zsend.at[s, i], zrecv.at[s, i], at_z(o, ry), OWN)
        summed[s].append(i)

    def reduce_c(b, s):
        arrived("oc", s, b)
        total = core_own[s, b] + core_recv[s, b]
        if (b, s) in DIRECT_REDUCE:
            for k, o in enumerate(OFFSETS[b]):
                for ry in range(2):
                    i = ry * Q + k * OWN
                    if o or ry:
                        send_z(s, o, ry, total[i : i + OWN])
                    else:
                        fin_own[s] = total[i : i + OWN]
        else:
            ylo_send[s, b] = total[Q:].astype(bf16)
            send(("oy", s, b), ylo_send.at[s, b], ylo_recv.at[s, b], at_z(0, 1), Q)
            core_own[s, b, pl.ds(0, Q), :] = total[:Q]

    def reduce_y(b, s):
        if (b, s) in DIRECT_REDUCE:
            return
        arrived("oy", s, b)
        total = core_own[s, b, pl.ds(0, Q), :] + ylo_recv[s, b].astype(f32)
        for k, o in enumerate(OFFSETS[b]):
            rows = total[k * OWN : (k + 1) * OWN]
            if o:
                send_z(s, o, 0, rows)
            else:
                fin_own[s] = rows

    summed = [[], []]

    def finish(s):
        arrived("oz", s)
        total = fin_own[s]
        for i in sorted(summed[s]):
            total = total + zrecv[s, i].astype(f32)
        (out_ref, ing_ref)[s][...] = total.astype(bf16)

    def weight_grad(s, m):
        left, right = (acts, mids) if s == 0 else (mids, acts)
        rows = pl.ds(m * TM, TM)
        (wing_ref, woutg_ref)[s][rows, :] = lax.dot_general(
            left[0, :, rows], right[1], (((0,), (0,)), ((), ())), preferred_element_type=f32
        ).astype(bf16)

    items = [(b, 0) for b in range(NB)] + [(b, 1) for b in reversed(range(NB))]
    last = len(items) - 1
    program = [
        (-9, start_gather, (0, range(NB))),
        (GATHER_1, start_gather, (1, reversed(range(NB)))),
        (FINISH_0, finish, (0,)),
    ]
    for i, (b, s) in enumerate(items):
        for stage, lag in (
            (reduce_y, LAG_REDUCE_Y), (reduce_c, LAG_REDUCE_C), (second_product, LAG_SECOND),
            (forward_x, LAG_FORWARD_X), (forward_y, LAG_FORWARD_Y), (middle, LAG_MIDDLE),
            (reduce_x, LAG_REDUCE_X), (pass_on, LAG_PASS_ON), (first_product, 0.0),
            (gather_c, (LAG_GATHER_C, GATHER_C_1)[s]), (gather_y, (LAG_GATHER_Y, GATHER_Y_1)[s]),
        ):
            program.append((i + lag, stage, (b, s)))
    for m in range(W // TM):
        program.append((GRAD_AT_1[m], weight_grad, (1, m)))
        program.append((GRAD_AT_0[m], weight_grad, (0, m)))
    for _, stage, args in sorted(program, key=lambda entry: entry[0]):
        stage(*args)
    finish(1)
    all_left()
    assert (len(landing), len(leaving)) == (N_LAND, N_LEAVE), (len(landing), len(leaving))


def block(tokens, w_in, w_out, cotangent):
    bf16, f32 = jnp.bfloat16, jnp.float32
    hbm = pl.BlockSpec(memory_space=pltpu.HBM)
    vmem = pl.BlockSpec(memory_space=pltpu.VMEM)
    weight = pltpu.VMEM((W, W), bf16)
    own = pltpu.VMEM((OWN, W), bf16)
    return pl.pallas_call(
        block_kernel,
        out_shape=(own, own, weight, weight),
        in_specs=[hbm] * 4,
        out_specs=(vmem,) * 4,
        scratch_shapes=[
            pltpu.VMEM((W, W), bf16),
            pltpu.VMEM((W, W), bf16),
            pltpu.VMEM((2, ROWS, W), bf16),
            pltpu.VMEM((2, NB, RB, W), f32),
            pltpu.VMEM((2, ROWS, W), bf16),
            pltpu.VMEM((2, NB, 6, YR, W), bf16),
            pltpu.VMEM((2, NB, YR, W), bf16),
            pltpu.VMEM((2, NB, YR, W), bf16),
            pltpu.VMEM((2, NB, 2, YR, W), f32),
            pltpu.VMEM((NB, YR, W), f32),
            pltpu.VMEM((2, ROWS, W), bf16),
            pltpu.VMEM((2, NB, 2 * Q, W), f32),
            pltpu.VMEM((2, NB, 2 * Q, W), f32),
            pltpu.VMEM((2, NB, 2 * Q, W), f32),
            pltpu.VMEM((RB, W), f32),
            pltpu.VMEM((2, NB, Q, W), bf16),
            pltpu.VMEM((2, NB, Q, W), bf16),
            pltpu.VMEM((2, OWN, W), f32),
            pltpu.VMEM((2, NZ * 2, OWN, W), bf16),
            pltpu.VMEM((2, NZ * 2, OWN, W), bf16),
            pltpu.SemaphoreType.DMA((4,)),
            pltpu.SemaphoreType.DMA((N_LEAVE,)),
            pltpu.SemaphoreType.DMA((N_LAND,)),
        ],
        compiler_params=pltpu.CompilerParams(
            collective_id=0, has_side_effects=True, vmem_limit_bytes=42 << 20
        ),
        cost_estimate=pl.CostEstimate(
            flops=12 * ROWS * W * W, bytes_accessed=12 << 20, transcendentals=0
        ),
        name="mlp_block",
    )(tokens, w_in, w_out, cotangent)


def on_device(tokens, w_in, w_out, cotangent):
    args = [pltpu.with_memory_space_constraint(a, pltpu.HBM) for a in (tokens, w_in, w_out, cotangent)]
    return block(*args)


def solution(mesh):
    in_specs = (P("tensor", "dp"), P("dp", "tensor"), P("tensor", "dp"), P("tensor", "dp"))
    out_specs = (P("tensor", "dp"), P("tensor", "dp"), P("dp", "tensor"), P("tensor", "dp"))
    return jax.shard_map(
        on_device, mesh=mesh, in_specs=in_specs, out_specs=out_specs, check_vma=False
    )
```

time: 520 us -> 85 us (0.16)
  waiting for transfers between devices: 461 us -> 0 us
  Pallas kernels: 0 us -> 79.9 us
  matrix products: 28.3 us -> 0 us
  between operations: 13.8 us -> 0.64 us
  other arithmetic: 6.8 us -> 0 us
    reduce_scatter x2 -> x0, waiting for transfers between devices: 208 us -> none  [the longest x1 116 us: on_device(): lax.psum_scatter(jnp.dot(rows, w_out, preferred_element_type=jnp.float32)...]
    all_gather x2 -> x0, waiting for transfers between devices: 130 us -> none  [the longest x1 69.4 us: on_device(): piece = lax.all_gather(cotangent, 'tensor', axis=0, tiled=True)]
    psum x1 -> x0, waiting for transfers between devices: 122 us -> none  [on_device(): hidden = lax.psum(partial_acc, 'dp')]
    pallas_call x0 -> x1, Pallas kernels: none -> 79.9 us  [block(): pl.pallas_call(block_kernel, out_shape=(own, own, weight, weight), in_spe...]
    dot_general x6 -> x0, matrix products: 28.3 us -> none  [the longest x2 9.73 us: contract_first(): lax.dot_general(left, right, (((0,), (0,)), ((), ())), preferred_element_...]
    convert_element_type x3 -> x0, other arithmetic: 6.8 us -> none  [the longest x1 3.79 us: on_device(): grad_hidden = (grad_activ * gelu_slope(hidden)).astype(jnp.bfloat16)]
  transfers between devices with their start and end apart: 5 -> 0, of which waited for: 5 -> 0; matrix products, arithmetic and copies ran while one was open for 5% -> 0% of each run, Pallas kernels for 0% -> 0%
where the time goes in v2:
time: 85 us; the launch traced here: 84.8 us
  Pallas kernels  79.9 us (94%)
  local copies, waits for them, and re-layouts  4.24 us (5%)
    pallas_call x1, Pallas kernels, block(): pl.pallas_call(block_kernel, out_shape=(own, own, weight, weight), in_spe...  79.9 us
    unnamed x4, local copies, waits for them, and re-layouts  4.24 us

profile of v2, /device:TPU:1, one launch (start us, length us, event | category | flops | bytes accessed | tf_op | source)
XLA Modules:
  0.0 84.8 jit_solution(16803392871707934308)
XLA Ops:
  0.6 79.9 %mlp_block.1 = (bf16[16,1152]{1,0:T(8,128)(2,1)S(1)}, bf16[16,1152]{1,0:T(8,128)(2,1)S(1)}, bf16[1152,1152]{1,0:T(8,128)(2,1)S(1)}, bf16[1152,1152]{1,0:T(8,128)(2,1)S(1)}) custom-call(bf16[16,1152]{1,0:T(8,128)(2,1)} %tok_hbm.1, bf16[1152,1152]{1,0:T(8,128)(2,1)} %win_hbm.1, bf16[1152,1152]{1,0:T(8,128)(2,1)} %wout_hbm.1, bf16[16,1152]{1,0:T(8,128)(2,1)} %cot_hbm.1), custom_call_target="tpu_custom_call" | custom-call | flops 8153726976 | bytes 12582912 | tf_op jit(solution)/shard_map/mlp_block/pallas_call | solution.py:324
  80.6 0.6 copy.12
  81.2 0.6 copy.13
  81.8 1.5 %copy.14 = bf16[1152,1152]{1,0:T(8,128)(2,1)} copy(bf16[1152,1152]{1,0:T(8,128)(2,1)S(1)} %get-tuple-element.6) | data formatting | bytes 5308416
  83.3 1.5 %copy.15 = bf16[1152,1152]{1,0:T(8,128)(2,1)} copy(bf16[1152,1152]{1,0:T(8,128)(2,1)S(1)} %get-tuple-element.7) | data formatting | bytes 5308416

commit v3 on v2

--- a/solution.py
+++ b/solution.py
@@ -1,4 +1,3 @@
-import functools
 import math
 
 import jax
@@ -21,8 +20,9 @@
 OFFSETS = [[0, 1], [7, 2], [6, 3], [5, 4]]
 Q = RB // 4
 TN = 384
+STORE_ROWS = 288
 TM = 128
-N_LAND, N_LEAVE = 95, 13
+N_LEAVE = 13
 
 
 def gelu_value(v):
@@ -33,17 +33,32 @@
     cdf = 0.5 * (1.0 + lax.erf(v * (1.0 / math.sqrt(2.0))))
     return cdf + v * jnp.exp(-0.5 * v * v) * (1.0 / math.sqrt(2.0 * math.pi))
 
-LAG_GATHER_Y, LAG_GATHER_C = -1.5, -0.1
-GATHER_Y_1, GATHER_C_1 = -1.5, -0.1
-LAG_PASS_ON, LAG_REDUCE_X, LAG_MIDDLE = 1.9, 3.8, 5.7
-LAG_FORWARD_Y, LAG_FORWARD_X, LAG_SECOND = 7.6, 9.5, 11.5
-LAG_REDUCE_C, LAG_REDUCE_Y = 12.4, 14.3
-FINISH_0 = 20.0
-GRAD_AT_1 = [15.45 + 0.5 * m for m in range(W // TM)]
-GRAD_AT_0 = [19.46] * 3 + [20.5] * 6
-GATHER_1 = -0.05
-DIRECT_GATHER = {(0, 0), (1, 0)}
+ORDER = [
+    ("sg", 0, 0), ("sg", 1, 0), ("sg", 2, 0), ("sg", 3, 0), ("gy", 0, 0), ("gy", 1, 0),
+    ("gy", 2, 0), ("sg", 2, 1), ("gc", 0, 0), ("gy", 3, 0), ("sg", 3, 1), ("p1", 0, 0),
+    ("gc", 1, 0), ("sg", 1, 1), ("sg", 0, 1), ("gc", 2, 0), ("p1", 1, 0), ("p1", 2, 0),
+    ("gc", 3, 0), ("gy", 2, 1), ("po", 0, 0), ("p1", 3, 0), ("gy", 1, 1), ("gy", 0, 1),
+    ("po", 1, 0), ("gy", 3, 1), ("po", 2, 0), ("gc", 2, 1), ("p1", 2, 1), ("gc", 1, 1),
+    ("po", 3, 0), ("rx", 0, 0), ("gc", 0, 1), ("p1", 1, 1), ("rx", 1, 0), ("rx", 2, 0),
+    ("p1", 0, 1), ("gc", 3, 1), ("po", 2, 1), ("mi", 0, 0), ("p1", 3, 1), ("rx", 3, 0),
+    ("po", 1, 1), ("mi", 1, 0), ("mi", 2, 0), ("po", 0, 1), ("fy", 0, 0), ("rx", 2, 1),
+    ("fr", 0, 0), ("mi", 3, 0), ("po", 3, 1), ("fy", 1, 0), ("fy", 2, 0), ("rx", 1, 1),
+    ("fr", 1, 0), ("mi", 2, 1), ("fr", 2, 0), ("rx", 0, 1), ("fy", 3, 0), ("fl", 0, 0),
+    ("mi", 1, 1), ("fr", 3, 0), ("rx", 3, 1), ("fl", 1, 0), ("fy", 2, 1), ("fl", 2, 0),
+    ("mi", 0, 1), ("fl", 3, 0), ("fr", 2, 1), ("p2", 0, 0), ("fy", 1, 1), ("mi", 3, 1),
+    ("p2", 1, 0), ("rc", 0, 0), ("fl", 2, 1), ("fr", 1, 1), ("fy", 0, 1), ("p2", 2, 0),
+    ("rc", 1, 0), ("fr", 0, 1), ("p2", 3, 0), ("rc", 2, 0), ("fl", 1, 1), ("wg", 0, 1),
+    ("fy", 3, 1), ("wg", 1, 1), ("wg", 2, 1), ("wg", 3, 1), ("ry", 0, 0), ("fr", 3, 1),
+    ("rc", 3, 0), ("p2", 2, 1), ("fl", 0, 1), ("wg", 4, 1), ("ry", 1, 0), ("wg", 5, 1),
+    ("wg", 6, 1), ("p2", 1, 1), ("ry", 2, 0), ("fl", 3, 1), ("rc", 2, 1), ("wg", 7, 1),
+    ("wg", 8, 1), ("ry", 3, 0), ("p2", 0, 1), ("rc", 1, 1), ("p2", 3, 1), ("ry", 2, 1),
+    ("rc", 0, 1), ("rc", 3, 1), ("ry", 1, 1), ("fi", 0), ("ry", 3, 1), ("wg", 0, 0), ("wg", 1, 0),
+    ("wg", 2, 0), ("wg", 3, 0), ("wg", 4, 0), ("wg", 5, 0), ("wg", 6, 0), ("wg", 7, 0),
+    ("wg", 8, 0), ("fi", 1),
+]
+DIRECT_GATHER = set()
 DIRECT_REDUCE = {(0, 1)}
+N_LAND = 2 + 12 * 2 * NB - len(DIRECT_GATHER) - len(DIRECT_REDUCE)
 DIAGONAL = {
     f % NZ for b, _ in DIRECT_GATHER | DIRECT_REDUCE for o in OFFSETS[b] for f in (o, -o) if o
 }
@@ -130,15 +145,13 @@
     def rows_at(b, rc, ry, k=0):
         return b * RB + rc * (RB // 2) + ry * (RB // 4) + k * OWN
 
-    def start_gather(s, blocks):
-        loads[s].wait()
+    def start_gather(b, s):
         src = acts.at[s, pl.ds(0, OWN)]
-        for b in blocks:
-            for k, o in enumerate(OFFSETS[b]):
-                for ry in range(2):
-                    if (o or ry) and (ry == 0 or (b, s) in DIRECT_GATHER):
-                        dst = acts.at[s, pl.ds(rows_at(b, 0, ry, k), OWN)]
-                        send(("gz", s, b), src, dst, at_z(NZ - o, ry), OWN)
+        for k, o in enumerate(OFFSETS[b]):
+            for ry in range(2):
+                if (o or ry) and (ry == 0 or (b, s) in DIRECT_GATHER):
+                    dst = acts.at[s, pl.ds(rows_at(b, 0, ry, k), OWN)]
+                    send(("gz", s, b), src, dst, at_z(NZ - o, ry), OWN)
 
     def gather_y(b, s):
         if (b, s) in DIRECT_GATHER:
@@ -217,10 +230,12 @@
         send(("a3", s, b), here, here, at_x(1), YR)
         send(("a2", s, b), here, here, at_x(3), YR)
 
-    def forward_x(b, s):
+    def forward_right(b, s):
         arrived("a1", s, b)
         here = mids.at[s, half(b, (x + 3) % NX, yh)]
         send(("a3", s, b), here, here, at_x(1), YR)
+
+    def forward_left(b, s):
         arrived("a2", s, b)
         here = mids.at[s, half(b, (x + 1) % NX, 1 - yh)]
         send(("a3", s, b), here, here, at_x(3), YR)
@@ -283,34 +298,23 @@
             total = total + zrecv[s, i].astype(f32)
         (out_ref, ing_ref)[s][...] = total.astype(bf16)
 
-    def weight_grad(s, m):
+    def weight_grad(m, s):
         left, right = (acts, mids) if s == 0 else (mids, acts)
         rows = pl.ds(m * TM, TM)
         (wing_ref, woutg_ref)[s][rows, :] = lax.dot_general(
             left[0, :, rows], right[1], (((0,), (0,)), ((), ())), preferred_element_type=f32
         ).astype(bf16)
 
-    items = [(b, 0) for b in range(NB)] + [(b, 1) for b in reversed(range(NB))]
-    last = len(items) - 1
-    program = [
-        (-9, start_gather, (0, range(NB))),
-        (GATHER_1, start_gather, (1, reversed(range(NB)))),
-        (FINISH_0, finish, (0,)),
-    ]
-    for i, (b, s) in enumerate(items):
-        for stage, lag in (
-            (reduce_y, LAG_REDUCE_Y), (reduce_c, LAG_REDUCE_C), (second_product, LAG_SECOND),
-            (forward_x, LAG_FORWARD_X), (forward_y, LAG_FORWARD_Y), (middle, LAG_MIDDLE),
-            (reduce_x, LAG_REDUCE_X), (pass_on, LAG_PASS_ON), (first_product, 0.0),
-            (gather_c, (LAG_GATHER_C, GATHER_C_1)[s]), (gather_y, (LAG_GATHER_Y, GATHER_Y_1)[s]),
-        ):
-            program.append((i + lag, stage, (b, s)))
-    for m in range(W // TM):
-        program.append((GRAD_AT_1[m], weight_grad, (1, m)))
-        program.append((GRAD_AT_0[m], weight_grad, (0, m)))
-    for _, stage, args in sorted(program, key=lambda entry: entry[0]):
-        stage(*args)
-    finish(1)
+    stages = {
+        "sg": start_gather, "gy": gather_y, "gc": gather_c, "p1": first_product,
+        "po": pass_on, "rx": reduce_x, "mi": middle, "fy": forward_y, "fr": forward_right,
+        "fl": forward_left, "p2": second_product, "rc": reduce_c, "ry": reduce_y,
+        "wg": weight_grad, "fi": finish,
+    }
+    for load in loads[:2]:
+        load.wait()
+    for name, *args in ORDER:
+        stages[name](*args)
     all_left()
     assert (len(landing), len(leaving)) == (N_LAND, N_LEAVE), (len(landing), len(leaving))
 
@@ -361,9 +365,38 @@
     )(tokens, w_in, w_out, cotangent)
 
 
+def store_kernel(*refs):
+    n = len(refs) // 2
+    sems = refs[-1]
+    copies = []
+    for source, target in zip(refs[:n], refs[n:-1]):
+        for rows in range(0, source.shape[0], STORE_ROWS):
+            piece = pl.ds(rows, min(STORE_ROWS, source.shape[0]))
+            copies.append(
+                pltpu.make_async_copy(source.at[piece], target.at[piece], sems.at[len(copies)])
+            )
+    for copy in copies:
+        copy.start()
+    for copy in copies:
+        copy.wait()
+
+
+def store(*arrays):
+    hbm = pl.BlockSpec(memory_space=pltpu.HBM)
+    return pl.pallas_call(
+        store_kernel,
+        out_shape=tuple(jax.ShapeDtypeStruct(a.shape, a.dtype) for a in arrays),
+        in_specs=[pl.BlockSpec(memory_space=pltpu.VMEM)] * len(arrays),
+        out_specs=(hbm,) * len(arrays),
+        scratch_shapes=[pltpu.SemaphoreType.DMA((2 + 2 * W // STORE_ROWS,))],
+        compiler_params=pltpu.CompilerParams(vmem_limit_bytes=1 << 20),
+        name="store",
+    )(*arrays)
+
+
 def on_device(tokens, w_in, w_out, cotangent):
     args = [pltpu.with_memory_space_constraint(a, pltpu.HBM) for a in (tokens, w_in, w_out, cotangent)]
-    return block(*args)
+    return store(*block(*args))
 
 
 def solution(mesh):

time: 85 us -> 79.7 us (0.938); the launches traced: 84.8 us -> 78.3 us
  local copies, waits for them, and re-layouts: 4.24 us -> 0 us
  Pallas kernels: 79.9 us -> 77.5 us
    pallas_call x1, Pallas kernels: 79.9 us -> 75 us  [block(): pl.pallas_call(block_kernel, out_shape=(own, own, weight, weight), in_spe...]
    unnamed x4 -> x0, local copies, waits for them, and re-layouts: 4.24 us -> none
    pallas_call x0 -> x1, Pallas kernels: none -> 2.48 us  [store(): pl.pallas_call(store_kernel, out_shape=tuple((jax.ShapeDtypeStruct(a.shap...]
where the time goes in v3:
time: 79.7 us; the launch traced here: 78.3 us
  Pallas kernels  77.5 us (97%)
  between operations  0.8 us (1%)
    pallas_call x1, Pallas kernels, block(): pl.pallas_call(block_kernel, out_shape=(own, own, weight, weight), in_spe...  75 us
    pallas_call x1, Pallas kernels, store(): pl.pallas_call(store_kernel, out_shape=tuple((jax.ShapeDtypeStruct(a.shap...  2.48 us

profile of v3, /device:TPU:1, one launch (start us, length us, event | category | flops | bytes accessed | tf_op | source)
XLA Modules:
  0.0 78.3 jit_solution(9809220280777646824)
XLA Ops:
  0.6 75.0 %mlp_block.1 = (bf16[16,1152]{1,0:T(8,128)(2,1)S(1)}, bf16[16,1152]{1,0:T(8,128)(2,1)S(1)}, bf16[1152,1152]{1,0:T(8,128)(2,1)S(1)}, bf16[1152,1152]{1,0:T(8,128)(2,1)S(1)}) custom-call(bf16[16,1152]{1,0:T(8,128)(2,1)} %tok_hbm.1, bf16[1152,1152]{1,0:T(8,128)(2,1)} %win_hbm.1, bf16[1152,1152]{1,0:T(8,128)(2,1)} %wout_hbm.1, bf16[16,1152]{1,0:T(8,128)(2,1)} %cot_hbm.1), custom_call_target="tpu_custom_call" | custom-call | flops 8153726976 | bytes 12582912 | tf_op jit(solution)/shard_map/mlp_block/pallas_call | solution.py:328
  75.6 2.5 %store.1 = (bf16[16,1152]{1,0:T(8,128)(2,1)}, bf16[16,1152]{1,0:T(8,128)(2,1)}, bf16[1152,1152]{1,0:T(8,128)(2,1)}, bf16[1152,1152]{1,0:T(8,128)(2,1)}) custom-call(bf16[16,1152]{1,0:T(8,128)(2,1)S(1)} %get-tuple-element.8.refs_0_, bf16[16,1152]{1,0:T(8,128)(2,1)S(1)} %get-tuple-element.9.refs_1_, bf16[1152,1152]{1,0:T(8,128)(2,1)S(1)} %get-tuple-element.10.refs_2_, ...), custom_call_target="tpu_custom_call" | custom-call | tf_op jit(solution)/shard_map/store/pallas_call | solution.py:386

commit v4 on v3

--- a/solution.py
+++ b/solution.py
@@ -17,7 +17,7 @@
 KO = NZ // NB
 XR = RB // NX
 YR = XR // NYH
-OFFSETS = [[0, 1], [7, 2], [6, 3], [5, 4]]
+OFFSETS = [[0, 1], [6, 3], [5, 4], [7, 2]]
 Q = RB // 4
 TN = 384
 STORE_ROWS = 288
@@ -52,12 +52,12 @@
     ("rc", 3, 0), ("p2", 2, 1), ("fl", 0, 1), ("wg", 4, 1), ("ry", 1, 0), ("wg", 5, 1),
     ("wg", 6, 1), ("p2", 1, 1), ("ry", 2, 0), ("fl", 3, 1), ("rc", 2, 1), ("wg", 7, 1),
     ("wg", 8, 1), ("ry", 3, 0), ("p2", 0, 1), ("rc", 1, 1), ("p2", 3, 1), ("ry", 2, 1),
-    ("rc", 0, 1), ("rc", 3, 1), ("ry", 1, 1), ("fi", 0), ("ry", 3, 1), ("wg", 0, 0), ("wg", 1, 0),
+    ("rc", 0, 1), ("rc", 3, 1), ("ry", 1, 1), ("ry", 0, 1), ("fi", 0), ("ry", 3, 1), ("wg", 0, 0), ("wg", 1, 0),
     ("wg", 2, 0), ("wg", 3, 0), ("wg", 4, 0), ("wg", 5, 0), ("wg", 6, 0), ("wg", 7, 0),
     ("wg", 8, 0), ("fi", 1),
 ]
 DIRECT_GATHER = set()
-DIRECT_REDUCE = {(0, 1)}
+DIRECT_REDUCE = set()
 N_LAND = 2 + 12 * 2 * NB - len(DIRECT_GATHER) - len(DIRECT_REDUCE)
 DIAGONAL = {
     f % NZ for b, _ in DIRECT_GATHER | DIRECT_REDUCE for o in OFFSETS[b] for f in (o, -o) if o

time: 79.7 us -> 78.9 us (0.990); the launches traced: 78.3 us -> 78.6 us
  no operation moved by 1% of the time
where the time goes in v4:
time: 78.9 us; the launch traced here: 78.6 us
  Pallas kernels  77.8 us (99%)
  between operations  0.8 us (1%)
    pallas_call x1, Pallas kernels, block(): pl.pallas_call(block_kernel, out_shape=(own, own, weight, weight), in_spe...  75.3 us
    pallas_call x1, Pallas kernels, store(): pl.pallas_call(store_kernel, out_shape=tuple((jax.ShapeDtypeStruct(a.shap...  2.48 us

profile of v4, /device:TPU:1, one launch (start us, length us, event | category | flops | bytes accessed | tf_op | source)
XLA Modules:
  0.0 78.6 jit_solution(940036872785338360)
XLA Ops:
  0.6 75.3 %mlp_block.1 = (bf16[16,1152]{1,0:T(8,128)(2,1)S(1)}, bf16[16,1152]{1,0:T(8,128)(2,1)S(1)}, bf16[1152,1152]{1,0:T(8,128)(2,1)S(1)}, bf16[1152,1152]{1,0:T(8,128)(2,1)S(1)}) custom-call(bf16[16,1152]{1,0:T(8,128)(2,1)} %tok_hbm.1, bf16[1152,1152]{1,0:T(8,128)(2,1)} %win_hbm.1, bf16[1152,1152]{1,0:T(8,128)(2,1)} %wout_hbm.1, bf16[16,1152]{1,0:T(8,128)(2,1)} %cot_hbm.1), custom_call_target="tpu_custom_call" | custom-call | flops 8153726976 | bytes 12582912 | tf_op jit(solution)/shard_map/mlp_block/pallas_call | solution.py:328
  76.0 2.5 %store.1 = (bf16[16,1152]{1,0:T(8,128)(2,1)}, bf16[16,1152]{1,0:T(8,128)(2,1)}, bf16[1152,1152]{1,0:T(8,128)(2,1)}, bf16[1152,1152]{1,0:T(8,128)(2,1)}) custom-call(bf16[16,1152]{1,0:T(8,128)(2,1)S(1)} %get-tuple-element.8.refs_0_, bf16[16,1152]{1,0:T(8,128)(2,1)S(1)} %get-tuple-element.9.refs_1_, bf16[1152,1152]{1,0:T(8,128)(2,1)S(1)} %get-tuple-element.10.refs_2_, ...), custom_call_target="tpu_custom_call" | custom-call | tf_op jit(solution)/shard_map/store/pallas_call | solution.py:386
